TPU v7x, 32 devices: a whole 2x2x4 slice. The times are simulated.
32 devices in a mesh: dp: 2 (over core), blk: 4 (over y, x), tensor: 4 (over z).
Axes of the slice: x: 2, y: 2, z: 4, core: 2. Of those that a mesh axis runs over, the one named last changes fastest.
Arguments:
- tokens: bfloat16 [4, 2048, 768], P('dp', 'blk', 'tensor'), may hold values from -6 to 6
- segment_ids: int32 [4, 2048], P('dp', 'blk'), may hold values from 0 to 2047, as said below
- input_weight: bfloat16 [3, 768, 768], P(None, None, 'tensor'), may hold values from -0.21875 to 0.21875
- input_bias: float32 [2, 768], P(None, 'tensor'), may hold values from -3 to 3
- output_weight: bfloat16 [768, 768], P('tensor'), may hold values from -1.75 to 1.75
- output_bias: float32 [768], replicated, may hold values from -3 to 3
- first_gain: float32 [768], replicated, may hold values from 0.5 to 1.5
- first_shift: float32 [768], replicated, may hold values from -3 to 3
- up_weight: bfloat16 [768, 3072], P(None, 'tensor'), may hold values from -0.21875 to 0.21875
- up_bias: float32 [3072], P('tensor'), may hold values from -3 to 3
- down_weight: bfloat16 [3072, 768], P('tensor'), may hold values from -0.109375 to 0.109375
- down_bias: float32 [768], replicated, may hold values from -3 to 3
- second_gain: float32 [768], replicated, may hold values from 0.5 to 1.5
- second_shift: float32 [768], replicated, may hold values from -3 to 3
- cotangent: bfloat16 [4, 2048, 768], P('dp', 'blk', 'tensor'), may hold values from -6 to 6
Outputs:
- layer_output: bfloat16 [4, 2048, 768], P('dp', 'blk', 'tensor')
- tokens_grad: float32 [4, 2048, 768], P('dp', 'blk', 'tensor')
- input_weight_grad: float32 [3, 768, 768], P(None, None, 'tensor')
- input_bias_grad: float32 [2, 768], P(None, 'tensor')
- output_weight_grad: float32 [768, 768], P('tensor')
- output_bias_grad: float32 [768], replicated
- first_gain_grad: float32 [768], replicated
- first_shift_grad: float32 [768], replicated
- up_weight_grad: float32 [768, 3072], P(None, 'tensor')
- up_bias_grad: float32 [3072], P('tensor')
- down_weight_grad: float32 [3072, 768], P('tensor')
- down_bias_grad: float32 [768], replicated
- second_gain_grad: float32 [768], replicated
- second_shift_grad: float32 [768], replicated
Inputs may be any that keep to these rules, and one draw needn't show every extreme that they name: `segment_ids`: tokens with equal ids form one document. Passages are contiguous runs about 144 tokens long, and each passage's id is the position of its first token, except that one document per row, with id 0, is made of the row's first passage, the passage that holds position 2046 and some passages between them. The row's last position, 2047, is a passage of its own with that id.
All inputs are finite; a program needn't handle non-finite values.
Results may differ from a plain program's by a relative error of at most 0.022.
Values may be sent and summed in bfloat16 or wider, within the bound.
A program may use at most 128 MiB of HBM per device.

v0:
```python
import functools

import jax
import jax.numpy as jnp
from jax import lax
from jax.experimental import pallas as pl
from jax.experimental.pallas import tpu as pltpu
from jax.sharding import PartitionSpec as P

HEAD_DIM = 64
EPS = 1e-12
MASKED = -1e30
MESH = pl.DeviceIdType.MESH
bf16 = jnp.bfloat16
f32 = jnp.float32
VMEM_LIMIT = 60 * 2**20


def dot(a, b, ca, cb):
    return lax.dot_general(a, b, (((ca,), (cb,)), ((), ())), preferred_element_type=f32)


def aligned(index, size):
    return pl.multiple_of(index * size, size)


def cut(index, size):
    return pl.ds(aligned(index, size), size)


class Refs:
    def __init__(self, names, refs):
        for name, ref in zip(names, refs, strict=True):
            setattr(self, name, ref)


class Sems:
    def __init__(self, ref=None):
        self.ref = ref
        self.used = 0

    def take(self, count):
        first = self.used
        self.used += count
        return first


class Swap:
    def __init__(self, sems, axis, n, src, dst, xor=False, stride=1):
        self.sems, self.axis, self.n, self.src, self.dst, self.xor = sems, axis, n, src, dst, xor
        self.stride = stride
        self.me = lax.axis_index(axis)
        self.send, self.recv = sems.take(n), sems.take(n)

    def to(self, k):
        return self.me ^ (k * self.stride) if self.xor else lax.rem(self.me + k, self.n)

    def source(self, k):
        return self.me ^ (k * self.stride) if self.xor else lax.rem(self.me + self.n - k, self.n)

    def copy(self, k, dst_index):
        return pltpu.make_async_remote_copy(
            self.src(self.to(k)),
            self.dst(dst_index),
            self.sems.ref.at[self.send + k],
            self.sems.ref.at[self.recv + k],
            device_id={self.axis: self.to(k)},
            device_id_type=MESH,
        )

    def start_one(self, k):
        self.copy(k, self.me).start()

    def start(self):
        each(1, self.n, self.start_one)

    def wait(self, k):
        self.copy(k, self.source(k)).wait_recv()

    def wait_all(self):
        each(1, self.n, self.wait)

    def done(self):
        each(1, self.n, lambda k: self.copy(k, self.me).wait_send())


def each(low, high, body):
    if high - low <= 4:
        for k in range(low, high):
            body(k)
    else:

        def step(k, carry):
            body(k)
            return carry

        lax.fori_loop(low, high, step, 0)


class Line:
    def __init__(self, sems, n, view, own):
        self.sems, self.n, self.view, self.own = sems, n, view, own
        self.t = lax.axis_index("tensor")
        self.recv, self.right, self.left = sems.take(n), sems.take(n), sems.take(n)

    def copy(self, chunk, right, k):
        return pltpu.make_async_remote_copy(
            self.own if k == 0 else self.view(chunk),
            self.view(chunk),
            self.sems.ref.at[(self.right if right else self.left) + k],
            self.sems.ref.at[self.recv + chunk],
            device_id={"tensor": self.t + 1 if right else self.t - 1},
            device_id_type=MESH,
        )

    def start(self):
        t, n = self.t, self.n
        pl.when(t < n - 1)(lambda: self.copy(t, True, 0).start())
        pl.when(t > 0)(lambda: self.copy(t, False, 0).start())

    def step(self, k):
        t, n = self.t, self.n

        @pl.when(t >= k)
        def _():
            self.copy(t - k, True, k).wait_recv()
            pl.when(t < n - 1)(lambda: self.copy(t - k, True, k).start())

        @pl.when(t + k < n)
        def _():
            self.copy(t + k, False, k).wait_recv()
            pl.when(t > 0)(lambda: self.copy(t + k, False, k).start())

    def done(self):
        t, n = self.t, self.n
        for k in range(n):
            pl.when((t >= k) & (t < n - 1))(lambda k=k: self.copy(t - k, True, k).wait_send())
            pl.when((t + k < n) & (t > 0))(lambda k=k: self.copy(t + k, False, k).wait_send())


class Plane:
    def __init__(self, sems, n, view, own):
        self.sems, self.n, self.view, self.own = sems, n, view, own
        self.b = lax.axis_index("blk")
        self.send, self.recv = sems.take(2 * n), sems.take(2 * n)

    def copy(self, k, half, origin, to, own):
        return pltpu.make_async_remote_copy(
            self.own(half) if own else self.view(origin, half),
            self.view(origin, half),
            self.sems.ref.at[self.send + 2 * k + half],
            self.sems.ref.at[self.recv + 2 * k + half],
            device_id={"blk": to},
            device_id_type=MESH,
        )

    def ours(self, k, half):
        return self.copy(k, half, self.b, self.b ^ k, True)

    def passed(self, half):
        origin, to = (self.b ^ 1, self.b ^ 2) if half == 0 else (self.b ^ 2, self.b ^ 1)
        return self.copy(3, half, origin, to, False)

    def start(self):
        if self.n == 4:
            for k, half in ((1, 0), (2, 1), (1, 1), (2, 0)):
                self.ours(k, half).start()
        else:

            def go(k):
                self.ours(k, 0).start()
                self.ours(k, 1).start()

            each(1, self.n, go)

    def landed(self, k, half):
        self.copy(k, half, self.b ^ k, self.b ^ k, True).wait_recv()

    def forward(self):
        if self.n == 4:
            self.landed(1, 0)
            self.passed(0).start()
            self.landed(2, 1)
            self.passed(1).start()

    def wait(self, k):
        if self.n != 4:
            self.landed(k, 0)
            self.landed(k, 1)
        elif k == 1:
            self.landed(1, 1)
        elif k == 2:
            self.landed(2, 0)
        else:
            self.landed(3, 0)
            self.landed(3, 1)

    def wait_all(self):
        each(1, self.n, self.wait)

    def done(self):
        if self.n == 4:
            for k, half in ((1, 0), (2, 1), (1, 1), (2, 0)):
                self.ours(k, half).wait_send()
            self.passed(0).wait_send()
            self.passed(1).wait_send()
        else:

            def go(k):
                self.ours(k, 0).wait_send()
                self.ours(k, 1).wait_send()

            each(1, self.n, go)


class Spread:
    def __init__(self, sems, n, view):
        self.sems, self.n, self.view = sems, n, view
        self.b, self.t = lax.axis_index("blk"), lax.axis_index("tensor")
        self.send, self.recv = sems.take(8 * n), sems.take(8 * n)

    def copy(self, s, k, half, origin, to):
        ref = self.view(s, origin, half)
        return pltpu.make_async_remote_copy(
            ref,
            ref,
            self.sems.ref.at[self.send + 8 * s + 2 * k + half],
            self.sems.ref.at[self.recv + 8 * s + 2 * k + half],
            device_id={"blk": to},
            device_id_type=MESH,
        )

    def ours(self, s):
        return [self.copy(s, k, half, self.b, self.b ^ k) for k, half in ((1, 0), (2, 1), (1, 1), (2, 0))]

    def passed(self, s, half):
        near, far = (1, 2) if half == 0 else (2, 1)
        return self.copy(s, 3, half, self.b ^ near, self.b ^ far)

    def landed(self, s, k, half):
        self.copy(s, k, half, self.b ^ k, self.b ^ k).wait_recv()

    def around(self, k, body):
        pl.when(self.t >= k)(lambda: body(self.t - k))
        pl.when(self.t + k < self.n)(lambda: body(self.t + k))

    def start(self, k):
        def body(s):
            for copy in self.ours(s):
                copy.start()

        self.around(k, body)

    def forward(self, k):
        def body(s):
            self.landed(s, 1, 0)
            self.passed(s, 0).start()
            self.landed(s, 2, 1)
            self.passed(s, 1).start()

        self.around(k, body)

    def wait_all(self):
        def body(s):
            self.landed(s, 1, 1)
            self.landed(s, 2, 0)
            self.landed(s, 3, 0)
            self.landed(s, 3, 1)

        for k in range(1, self.n):
            self.around(k, body)

    def done(self):
        def body(s):
            for copy in (*self.ours(s), self.passed(s, 0), self.passed(s, 1)):
                copy.wait_send()

        for k in range(1, self.n):
            self.around(k, body)


class Fold:
    def __init__(self, sems, part, relay, inbox):
        self.sems, self.part, self.relay, self.inbox = sems, part, relay, inbox
        self.b = lax.axis_index("blk")
        self.send, self.recv = sems.take(6), sems.take(6)

    def copy(self, n, src, dst, k):
        return pltpu.make_async_remote_copy(
            src,
            dst,
            self.sems.ref.at[self.send + n],
            self.sems.ref.at[self.recv + n],
            device_id={"blk": self.b ^ k},
            device_id_type=MESH,
        )

    def across(self, half):
        return self.copy(half, self.part(self.b ^ 3, half), self.relay(half), half + 1)

    def near(self, half):
        return self.copy(2 + half, self.part(self.b ^ (half + 1), half), self.inbox(half), half + 1)

    def folded(self, half):
        return self.copy(4 + half, self.relay(half), self.inbox(2 + half), 2 - half)

    def fold(self, half):
        self.across(half).wait_recv()
        part, relay = self.part(self.b ^ (2 - half), half), self.relay(half)
        relay[...] = (part[...].astype(f32) + relay[...].astype(f32)).astype(bf16)
        self.folded(half).start()

    def wait(self, half):
        self.near(half).wait_recv()
        self.folded(half).wait_recv()

    def received(self, half):
        return self.inbox(half)[...].astype(f32) + self.inbox(2 + half)[...].astype(f32)

    def done(self):
        for half in (0, 1):
            for transfer in (self.across, self.near, self.folded):
                transfer(half).wait_send()


class LineFold:
    def __init__(self, sems, n, part, relay):
        self.sems, self.n, self.part, self.relay = sems, n, part, relay
        self.t = lax.axis_index("tensor")
        self.send, self.recv = sems.take(n), sems.take(n + 1)

    def copy(self, j, right, fresh):
        to = self.t + 1 if right else self.t - 1
        slot = j if right else jnp.where(j == to, self.n, j)
        return pltpu.make_async_remote_copy(
            self.part(j) if fresh else self.relay(j),
            self.relay(slot),
            self.sems.ref.at[self.send + j],
            self.sems.ref.at[self.recv + slot],
            device_id={"tensor": to},
            device_id_type=MESH,
        )

    def landed(self, slot):
        pltpu.make_async_remote_copy(
            self.relay(slot),
            self.relay(slot),
            self.sems.ref.at[self.send],
            self.sems.ref.at[self.recv + slot],
            device_id={"tensor": lax.rem(self.t + 1, self.n)},
            device_id_type=MESH,
        ).wait_recv()

    def start(self):
        n = self.n

        @pl.when(self.t == 0)
        def _():
            for j in range(n - 1, 0, -1):
                self.copy(j, True, True).start()

        @pl.when(self.t == n - 1)
        def _():
            for j in range(n - 1):
                self.copy(j, False, True).start()

    def pass_on(self, j, right):
        self.landed(j)
        relay, part = self.relay(j), self.part(j)
        relay[...] = (relay[...].astype(f32) + part[...].astype(f32)).astype(bf16)
        self.copy(j, right, False).start()

    def step(self, m):
        back = self.n - 1 - self.t
        pl.when((self.t >= 1) & (self.t <= m) & (back >= 1))(lambda: self.pass_on(self.n - 1 + self.t - m, True))
        pl.when((back >= 1) & (back <= m) & (self.t >= 1))(lambda: self.pass_on(m - back, False))

    def finish(self, store):
        @pl.when(self.t > 0)
        def _():
            self.landed(self.t)
            store(self.relay(self.t))

        @pl.when(self.t < self.n - 1)
        def _():
            self.landed(self.n)
            store(self.relay(self.n))

    def done(self):
        for j in range(self.n):
            pl.when(self.t < j)(lambda j=j: self.copy(j, True, False).wait_send())
            pl.when(self.t > j)(lambda j=j: self.copy(j, False, False).wait_send())


class Dims:
    def __init__(self, mesh, rows, tok, width, ff):
        self.z, self.nb, self.nc = mesh.shape["tensor"], mesh.shape["blk"], mesh.shape["dp"]
        self.rows, self.tok, self.lw, self.ff = rows, tok, width, ff
        self.d = width * self.z
        self.heads = width // HEAD_DIM
        self.pt = tok // self.z
        self.own = rows * self.pt
        self.hf = ff // 2
        self.hid = self.hf * self.z
        self.uq, self.dq, self.oq, self.ol = self.d // 4, self.hf // 4, width // 4, self.d // 2
        self.wr = 3 * width


def enter(dm, dp=True, blk=True, tensor=True):
    barrier = pltpu.get_barrier_semaphore()
    count = 0
    for axis, n, wanted in (("dp", dm.nc, dp), ("blk", dm.nb, blk), ("tensor", dm.z, tensor)):
        if not wanted:
            continue
        me = lax.axis_index(axis)

        def greet(k, axis=axis, n=n, me=me):
            pl.semaphore_signal(barrier, inc=1, device_id={axis: lax.rem(me + k, n)}, device_id_type=MESH)

        each(1, n, greet)
        count += n - 1
    pl.semaphore_wait(barrier, count)


def mask_bias(segg, r, key_block, own_block, tok):
    key_row = segg[key_block, r : r + 1, :]
    column = jnp.transpose(jnp.broadcast_to(key_row.astype(f32), (128, tok)))
    wide = jnp.concatenate([column] * (tok // 128), axis=1)
    query_row = segg[own_block, r : r + 1, :].astype(f32)
    return jnp.where(wide == query_row, 0.0, MASKED)


def layer_kernel(dm, names, *refs):
    R = Refs(names, refs)
    t, b, c = lax.axis_index("tensor"), lax.axis_index("blk"), lax.axis_index("dp")
    q = lax.rem(b, 4)
    sems = Sems(R.sems)
    rows, lw, pt, own, d, tok, hf, z = dm.rows, dm.lw, dm.pt, dm.own, dm.d, dm.tok, dm.hf, dm.z
    small = dm.nb == 4
    mine, other = cut(c, own), cut(1 - c, own)
    quarter = lambda i: lax.rem(i, 4)
    half_d, half_z, half_h = d // 2, z // 2, dm.hid // 2
    split_u, split_o = dm.uq // 2, 128

    def z_swap(src, dst):
        return Swap(sems, "tensor", z, src, dst)

    def pair(src, dst):
        return Swap(sems, "dp", dm.nc, src, dst)

    token_lines = [
        Line(sems, z, lambda i, r=r: R.xT.at[r, cut(i, lw), :], R.xT.at[r, cut(t, lw), :]) for r in range(rows)
    ]
    seg_swap = Swap(sems, "blk", dm.nb, lambda to: R.segg.at[b], lambda i: R.segg.at[i], xor=True)
    ub_swap = z_swap(lambda to: R.ub8, lambda i: R.ubH.at[:, cut(i, hf)])
    up_own = R.up.at[cut(q, dm.uq), cut(c, hf)]
    down_own = R.down.at[pl.ds(pl.multiple_of(hf * c + dm.dq * q, dm.dq), dm.dq), :]
    wo_own = R.wo.at[:, cut(c, dm.ol)]

    def up_piece(i):
        return R.upH.at[cut(q, dm.uq), cut(i, hf)]

    def down_piece(i):
        return R.downH.at[i, cut(q, dm.dq), :]

    def wo_piece(i):
        return R.woF.at[i, :, cut(c, dm.ol)]

    up_line = Line(sems, z, up_piece, up_own)
    down_line = Line(sems, z, down_piece, down_own)
    wo_line = Line(sems, z, wo_piece, wo_own)

    def up_view(s, i, half):
        start = pl.multiple_of(dm.uq * quarter(i) + split_u * half, split_u)
        return R.upH.at[pl.ds(start, split_u), cut(s, hf)]

    def down_view(s, i, half):
        return R.downH.at[s, cut(quarter(i), dm.dq), pl.ds(half_d * half, half_d)]

    up_spread, down_spread = Spread(sems, z, up_view), Spread(sems, z, down_view)
    wo_pair = pair(lambda to: R.woF.at[:, :, cut(c, dm.ol)], lambda i: R.woF.at[:, :, cut(i, dm.ol)])
    cot_swap = z_swap(lambda to: R.cot.at[:, :, cut(to, pt)], lambda i: R.cotT.at[:, cut(i, lw), :])
    kv_planes = [
        Plane(
            sems,
            dm.nb,
            lambda i, half, r=r: R.kv.at[r, i, pl.ds(lw * half, lw), :],
            lambda half, r=r: R.kv.at[r, b, pl.ds(lw * half, lw), :],
        )
        for r in range(rows)
    ]
    ctx_swaps = [
        z_swap(lambda to, r=r: R.ctxs.at[r, :, cut(to, pt)], lambda i, r=r: R.ctxT.at[r, cut(i, lw), :])
        for r in range(rows)
    ]
    hl_pair = pair(lambda to: R.hl.at[mine], lambda i: R.hl.at[cut(i, own)])
    feed_pair = pair(lambda to: R.fs_s.at[0], lambda i: R.fs_r.at[0])
    fg_pair = pair(lambda to: R.fgf.at[mine], lambda i: R.fgf.at[cut(i, own)])
    part_pair = pair(lambda to: R.fs_s.at[1], lambda i: R.fs_r.at[1])
    og_pair = pair(lambda to: R.og_s, lambda i: R.og_r)
    out_swaps = [
        z_swap(lambda to, r=r: R.outT.at[r, cut(to, lw), :], lambda i, r=r: R.loT.at[r, :, cut(i, pt)])
        for r in range(rows)
    ]
    grad_swaps = [
        z_swap(lambda to, r=r: R.cgT.at[r, cut(to, lw), :], lambda i, r=r: R.doT.at[r, :, cut(i, pt)])
        for r in range(rows)
    ]

    def u_part(i, half):
        return R.uG.at[cut(quarter(i), dm.uq), pl.ds(half_h * half, half_h)]

    def d_part(i, half):
        return R.dG.at[pl.ds(half_z * half, half_z), cut(quarter(i), dm.dq), :]

    def o_part(i, half):
        return R.oG.at[pl.ds(half_z * half, half_z), cut(quarter(i), dm.oq), :]

    parts = (u_part, d_part, o_part)
    first_stage = tuple(
        Fold(sems, part, lambda half, got=got: got.at[4 + half], lambda n, got=got: got.at[n])
        for part, got in zip(parts, (R.ur, R.dr, R.orr), strict=True)
    )
    second_stage = (
        LineFold(sems, z, lambda j: R.uG.at[cut(q, dm.uq), cut(j, hf)], lambda j: R.u2.at[j]),
        LineFold(sems, z, lambda j: R.dG.at[j, cut(q, dm.dq), :], lambda j: R.d2.at[j]),
        LineFold(sems, z, lambda j: R.oG.at[j, cut(q, dm.oq), :], lambda j: R.o2.at[j]),
    )
    groups = dm.nb // 4
    piece_refs, group_refs = (R.uP, R.dP, R.oP), (R.gu, R.gd, R.go)
    group_stage = tuple(
        Swap(sems, "blk", groups, lambda to, ref=ref: ref, lambda i, got=got: got.at[i // 4], True, 4)
        for ref, got in zip(piece_refs, group_refs, strict=True)
    )

    def fu_view(i, half):
        return R.fu.at[pl.ds(pl.multiple_of(dm.uq * quarter(i) + split_u * half, split_u), split_u), cut(c, hf)]

    def fd_view(i, half):
        start = pl.multiple_of(hf * c + dm.dq * quarter(i), dm.dq)
        return R.fd.at[pl.ds(start, dm.dq), pl.ds(half_d * half, half_d)]

    def fo_view(i, half):
        start = pl.multiple_of(dm.ol * c + split_o * half, 128)
        return R.fo.at[cut(quarter(i), dm.oq), pl.ds(start, dm.ol - split_o if half else split_o)]

    piece_halves = (
        lambda half: R.uP.at[pl.ds(split_u * half, split_u), :],
        lambda half: R.dP.at[:, pl.ds(half_d * half, half_d)],
        lambda half: R.oP.at[:, pl.ds(split_o * half, dm.ol - split_o if half else split_o)],
    )
    third_stage = tuple(
        Plane(sems, 4, view, piece) for view, piece in zip((fu_view, fd_view, fo_view), piece_halves, strict=True)
    )
    place = (
        R.fu.at[cut(q, dm.uq), cut(c, hf)],
        R.fd.at[pl.ds(pl.multiple_of(hf * c + dm.dq * q, dm.dq), dm.dq), :],
        R.fo.at[cut(q, dm.oq), cut(c, dm.ol)],
    )
    place_copies = [
        pltpu.make_async_copy(src, dst, R.local.at[4 + n])
        for n, (src, dst) in enumerate(zip(piece_refs, place, strict=True))
    ]
    last_stage = (
        pair(lambda to: R.fu.at[:, cut(c, hf)], lambda i: R.fu.at[:, cut(i, hf)]),
        pair(lambda to: R.fd.at[cut(c, hf), :], lambda i: R.fd.at[cut(i, hf), :]),
        pair(lambda to: R.fo.at[:, cut(c, dm.ol)], lambda i: R.fo.at[:, cut(i, dm.ol)]),
    )
    vec_pair = pair(lambda to: R.sv, lambda i: R.vp)
    vec_blk = Swap(sems, "blk", dm.nb, lambda to: R.vs.at[0], lambda i: R.vb.at[i], xor=True)
    vec_z = z_swap(lambda to: R.vs.at[1], lambda i: R.vz.at[i])
    bv_pair = pair(lambda to: R.bv_s.at[0], lambda i: R.bvp)
    bv_blk = Swap(sems, "blk", dm.nb, lambda to: R.bv_s.at[1], lambda i: R.bvb.at[i], xor=True)
    if small:
        kv_folds = [
            Fold(
                sems,
                lambda i, half, r=r: R.kv.at[r, i, pl.ds(lw * half, lw), :],
                lambda half, r=r: R.dkv_r.at[r, 2, pl.ds(lw * half, lw), :],
                lambda n, r=r: R.dkv_r.at[r, n // 2, pl.ds(lw * (n % 2), lw), :],
            )
            for r in range(rows)
        ]
    else:
        kv_folds = [
            Swap(sems, "blk", dm.nb, lambda to, r=r: R.kv.at[r, to], lambda i, r=r: R.dkv_r.at[r, i], xor=True)
            for r in range(rows)
        ]
    tok_folds = [
        LineFold(sems, z, lambda j, r=r: R.tp_s.at[r, cut(j, lw), :], lambda j, r=r: R.tp_r.at[r, j])
        for r in range(rows)
    ]
    half_w, wq_r, wq_l = dm.wr // 2, dm.wr // 4, d // 2
    w_pair = pair(lambda to: R.wT.at[cut(to, half_w), :], lambda i: R.wR)

    def w_at(i):
        return lax.div(quarter(i), 2), lax.rem(i, 2)

    w_blk = Swap(
        sems, "blk", 4,
        lambda to: R.w1.at[cut(w_at(to)[0], wq_r), cut(w_at(to)[1], wq_l)],
        lambda i: R.wr.at[quarter(i)], xor=True,
    )
    w_split = 80

    def wf_view(i, half):
        start = pl.multiple_of(half_w * c + wq_r * w_at(i)[0] + w_split * half, 16)
        return R.wF.at[pl.ds(start, wq_r - w_split if half else w_split), cut(w_at(i)[1], wq_l)]

    start_r, start_l = w_at(b)
    w_group = Swap(sems, "blk", groups, lambda to: R.wP, lambda i: R.gw.at[i // 4], True, 4)
    w_plane = Plane(
        sems, 4, wf_view, lambda half: R.wP.at[pl.ds(w_split * half, wq_r - w_split if half else w_split), :]
    )
    w_place = pltpu.make_async_copy(
        R.wP,
        R.wF.at[pl.ds(pl.multiple_of(half_w * c + wq_r * start_r, 16), wq_r), cut(start_l, wq_l)],
        R.local.at[7],
    )
    w_last = pair(lambda to: R.wF.at[cut(c, half_w), :], lambda i: R.wF.at[cut(i, half_w), :])

    def sync(src, dst):
        copy = pltpu.make_async_copy(src, dst, R.local.at[3])
        copy.start()
        copy.wait()

    def chunk_of(r, block):
        if small:
            return R.kv.at[r, block]
        sync(R.kv.at[r, block], R.kvc)
        return R.kvc

    def project(r):
        y = dot(R.w[...].reshape(dm.wr, d), R.xT[r], 1, 0)
        R.qT[r] = (y[:lw] + R.bcol[0][:, :1]).astype(bf16) * bf16(HEAD_DIM**-0.5)
        chunk = R.kv.at[r, b] if small else R.kvc
        chunk[0:lw, :] = y[lw : 2 * lw].astype(bf16)
        chunk[lw : 2 * lw, :] = (y[2 * lw :] + R.bcol[1][:, :1]).astype(bf16)
        if not small:
            sync(R.kvc, R.kv.at[r, b])
        for h in range(dm.heads):
            R.m_s[r, h] = jnp.full((8, tok), MASKED, f32)
            R.l_s[r, h] = jnp.zeros((8, tok), f32)
            R.acc[r, h] = jnp.zeros((HEAD_DIM, tok), f32)
        kv_planes[r].start()

    def attend(r, block):
        bias = mask_bias(R.segg, r, block, b, tok)
        chunk = chunk_of(r, block)
        for h in range(dm.heads):
            k = chunk[pl.ds(HEAD_DIM * h, HEAD_DIM), :]
            v = chunk[pl.ds(lw + HEAD_DIM * h, HEAD_DIM), :]
            s = dot(k, R.qT[r, pl.ds(HEAD_DIM * h, HEAD_DIM), :], 0, 0) + bias
            old = R.m_s[r, h, :1]
            new = jnp.maximum(old, jnp.max(s, 0, keepdims=True))
            p = jnp.exp(s - new)
            scale = jnp.exp(old - new)
            R.l_s[r, h, :1] = R.l_s[r, h, :1] * scale + jnp.sum(p, 0, keepdims=True)
            R.m_s[r, h, :1] = new
            R.acc[r, h] = R.acc[r, h] * scale + dot(v, p.astype(bf16), 1, 0)

    def attend_near(r, k):
        if small:
            kv_planes[r].wait(k)
            attend(r, b ^ k)

    def attend_rest(r):
        if not small:

            def body(k):
                kv_planes[r].wait(k)
                attend(r, b ^ k)

            each(1, dm.nb, body)

    def finish(r):
        for h in range(dm.heads):
            denominator = R.l_s[r, h, :1]
            ctx = R.acc[r, h] / denominator
            R.ctxr[r, pl.ds(HEAD_DIM * h, HEAD_DIM), :] = ctx
            R.ctxs[r, pl.ds(HEAD_DIM * h, HEAD_DIM), :] = ctx.astype(bf16)
            R.lse[r, h : h + 1, :] = R.m_s[r, h, :1] + jnp.log(denominator)
        R.ctxT[r, cut(t, lw), :] = R.ctxs[r, :, cut(t, pt)]
        ctx_swaps[r].start()

    enter(dm)
    for r in range(rows):
        R.xT[r, cut(t, lw), :] = R.tok[r]
    token_lines[0].start()
    up_line.start()
    weight_copies = [
        pltpu.make_async_copy(src, dst, R.local.at[n])
        for n, (src, dst) in enumerate(
            (
                (R.up.at[:, cut(c, hf)], R.upH.at[:, cut(t, hf)]),
                (R.down.at[cut(c, hf), :], R.downH.at[t]),
                (wo_own, wo_piece(t)),
            )
        )
    ]
    for copy in weight_copies:
        copy.start()
    for r in range(rows):
        R.cotT[r, cut(t, lw), :] = R.cot[r, :, cut(t, pt)]
    for m in range(3):
        R.wN[m] = jnp.transpose(R.w[m])
    R.segg[b] = jnp.zeros((8, tok), jnp.int32)
    R.segg[b, 0:rows, :] = R.seg[...]
    seg_swap.start()
    for n in range(7):
        R.vec[n, :] = getattr(R, f"vec{n}")[...]
    for n in range(2):
        R.bcol[n] = jnp.transpose(jnp.broadcast_to(R.ib[n : n + 1, :], (128, lw)))
    R.ub8[...] = jnp.broadcast_to(R.vec[6:7, cut(c, hf)], (8, hf))
    R.ubH[:, cut(t, hf)] = R.ub8[...]
    ub_swap.start()

    token_lines[0].step(1)
    up_line.step(1)
    up_spread.start(1)
    token_lines[0].step(2)
    token_lines[1].start()
    up_line.step(2)
    up_spread.start(2)
    token_lines[0].step(3)
    project(0)
    up_line.step(3)
    up_spread.start(3)
    up_spread.forward(1)
    token_lines[1].step(1)
    wo_line.start()
    seg_swap.wait_all()
    attend(0, b)
    up_spread.forward(2)
    token_lines[1].step(2)
    down_line.start()
    kv_planes[0].forward()
    up_spread.forward(3)
    wo_line.step(1)
    token_lines[1].step(3)
    project(1)
    wo_line.step(2)
    down_line.step(1)
    down_spread.start(1)
    attend(1, b)
    wo_line.step(3)
    for copy in weight_copies:
        copy.wait()
    wo_pair.start()
    attend_near(0, 1)
    down_line.step(2)
    down_spread.start(2)
    attend_near(0, 2)
    down_line.step(3)
    down_spread.start(3)
    attend_near(0, 3)
    attend_rest(0)
    finish(0)
    kv_planes[1].forward()
    attend_near(1, 1)
    down_spread.forward(1)
    attend_near(1, 2)
    down_spread.forward(2)
    attend_near(1, 3)
    attend_rest(1)
    finish(1)
    cot_swap.start()
    down_spread.forward(3)

    out_b, g1, s1, down_b, g2, s2 = (R.vec[n : n + 1, :] for n in range(6))

    def stats(x):
        center = x - jnp.mean(x, -1, keepdims=True)
        inverse = lax.rsqrt(jnp.mean(center * center, -1, keepdims=True) + EPS)
        return center * inverse, inverse

    def norm_back(g, gain, zn, inverse):
        e = g * gain
        return (e - jnp.mean(e, -1, keepdims=True) - zn * jnp.mean(e * zn, -1, keepdims=True)) * inverse

    def total(x):
        return jnp.sum(x, 0, keepdims=True)

    blocks = dm.hid // tok

    inverse1 = []
    wo_pair.wait_all()
    for r in range(rows):
        ctx_swaps[r].wait_all()
        attended = dot(R.ctxT[r], R.woF[...].reshape(d, d), 0, 0) + out_b
        zn, inv = stats(jnp.transpose(R.xT[r, :, cut(t, pt)].astype(f32)) + attended)
        inverse1.append(inv)
        R.z1_s[pl.ds(pt * r, pt), :] = zn
        R.hl[pl.ds(pl.multiple_of(own * c + pt * r, pt), pt), :] = (zn * g1 + s1).astype(bf16)
    hl_pair.start()
    ub_swap.wait_all()

    def expand(core):
        part = cut(core, own)
        for n in range(blocks):
            cols = pl.ds(tok * n, tok)
            v = dot(R.hl[part, :], R.upH[:, cols], 1, 0) + R.ubH[:1, cols]
            phi = 0.5 + 0.5 * lax.erf(v * (0.5**0.5))
            R.act[part, cols] = (v * phi).astype(bf16)
            R.pool[cut(2 * n + core, own), :] = phi + v * (jnp.exp(-0.5 * v * v) * 0.3989422804014327)

    up_spread.wait_all()
    expand(c)
    hl_pair.wait_all()
    expand(1 - c)
    down_spread.wait_all()
    down_w = R.downH[...].reshape(dm.hid, d)
    R.fs_s[0] = dot(R.act[other, :], down_w, 1, 0).astype(bf16)
    feed_pair.start()
    feed = dot(R.act[mine, :], down_w, 1, 0) + down_b
    cot_swap.wait_all()
    g = jnp.concatenate([jnp.transpose(R.cotT[r].astype(f32)) for r in range(rows)], 0)
    feed_pair.wait_all()
    hidden = R.z1_s[...] * g1 + s1
    z2, inverse2 = stats(hidden + (feed + R.fs_r[0].astype(f32)))
    resid = norm_back(g, g2, z2, inverse2)
    R.srg_s[...] = resid
    low = resid.astype(bf16)
    R.fgf[mine, :] = low
    fg_pair.start()
    out = z2 * g2 + s2
    R.sv[...] = jnp.zeros_like(R.sv)
    R.sv[0:1, :] = total(g * z2)
    R.sv[1:2, :] = total(g)
    R.sv[2:3, :] = total(low.astype(f32))

    def contract(core):
        part = cut(core, own)
        for n in range(blocks):
            cols = pl.ds(tok * n, tok)
            grad = dot(R.fgf[part, :], R.downH[...].reshape(dm.hid, d)[tok * n : tok * (n + 1)], 1, 1)
            R.bg[part, cols] = (grad * R.pool[cut(2 * n + core, own), :]).astype(bf16)

    contract(c)
    fg_pair.wait_all()
    contract(1 - c)
    R.fs_s[1] = dot(R.bg[other, :], R.upH[...], 1, 1).astype(bf16)
    part_pair.start()
    part = dot(R.bg[mine, :], R.upH[...], 1, 1)
    for r in range(rows):
        R.outT[r] = jnp.transpose(out[pt * r : pt * (r + 1)]).astype(bf16)
        R.loT[r, :, cut(t, pt)] = R.outT[r, cut(t, lw), :]
        out_swaps[r].start()

    def send_first(n):
        for half in (0, 1):
            first_stage[n].across(half).start()
        for half in (0, 1):
            first_stage[n].near(half).start()

    for n in range(z):
        R.dG[n] = dot(R.act[:, pl.ds(hf * n, hf)], R.fgf[...], 0, 0).astype(bf16)
    send_first(1)
    part_pair.wait_all()
    hidden_grad = R.srg_s[...] + (part + R.fs_r[1].astype(f32))
    z1 = R.z1_s[...]
    first = norm_back(hidden_grad, g1, z1, jnp.concatenate(inverse1, 0))
    low = first.astype(bf16)
    for r in range(rows):
        R.cgT[r] = dot(R.woF[...].reshape(d, d), low[pt * r : pt * (r + 1)], 1, 1).astype(bf16)
        R.doT[r, :, cut(t, pt)] = R.cgT[r, cut(t, lw), :]
        grad_swaps[r].start()
        R.frT[r] = jnp.transpose(first[pt * r : pt * (r + 1)])
    R.sv[3:4, :] = total(hidden_grad * z1)
    R.sv[4:5, :] = total(hidden_grad)
    R.sv[5:6, :] = total(low.astype(f32))
    out_grad = sum(dot(R.ctxT[r], low[pt * r : pt * (r + 1)], 1, 0) for r in range(rows))
    left = out_grad[:, : dm.ol].reshape(z, lw, dm.ol)
    right = out_grad[:, dm.ol :].reshape(z, lw, dm.ol)
    R.oG[...] = jnp.where(c == 0, left, right).astype(bf16)
    R.og_s[...] = jnp.where(c == 0, right, left).astype(bf16)
    og_pair.start()
    for n in range(blocks):
        cols = pl.ds(tok * n, tok)
        R.uG[:, cols] = dot(R.hl[...], R.bg[:, cols], 0, 0).astype(bf16)
    for n in range(z):
        R.sv[pl.ds(6 + 2 * c + n // 2, 1), pl.ds(hf * (n % 2), hf)] = total(
            R.bg[:, pl.ds(hf * n, hf)].astype(f32)
        )
    vec_pair.start()
    first_stage[1].fold(0)
    first_stage[1].fold(1)
    og_pair.wait_all()
    R.oG[...] = (R.oG[...].astype(f32) + R.og_r[...].astype(f32)).astype(bf16)

    for line in (*token_lines, up_line, down_line, wo_line):
        line.done()
    for r in range(rows):
        kv_planes[r].done()

    def store_chunk(r, block):
        if not small:
            sync(R.kvc, R.kv.at[r, block])

    def own_kv(r, at, size):
        return R.pool.at[pl.ds(2 * lw * r + at, size), :]

    def dq_at(r, at, size):
        return R.pool.at[pl.ds(2 * lw * rows + lw * r + at, size), :]

    def prepare(r):
        grad_swaps[r].wait_all()
        for h in range(dm.heads):
            feats = pl.ds(HEAD_DIM * h, HEAD_DIM)
            R.delta[r, h : h + 1, :] = jnp.sum(R.doT[r, feats, :].astype(f32) * R.ctxr[r, feats, :], 0, keepdims=True)
        dq_at(r, 0, lw)[...] = jnp.zeros((lw, tok), f32)

    def attend_back(r, block, keep):
        bias = mask_bias(R.segg, r, block, b, tok)
        chunk = chunk_of(r, block)
        for h in range(dm.heads):
            feats = pl.ds(HEAD_DIM * h, HEAD_DIM)
            more = pl.ds(lw + HEAD_DIM * h, HEAD_DIM)
            k, v = chunk[feats, :], chunk[more, :]
            qh, do = R.qT[r, feats, :], R.doT[r, feats, :]
            p = jnp.exp(dot(k, qh, 0, 0) + bias - R.lse[r, h : h + 1, :])
            ds = (p * (dot(v, do, 0, 0) - R.delta[r, h : h + 1, :])).astype(bf16)
            dq_at(r, HEAD_DIM * h, HEAD_DIM)[...] += dot(k, ds, 1, 0)
            dk, dv = dot(qh, ds, 1, 1), dot(do, p.astype(bf16), 1, 1)
            if keep:
                own_kv(r, HEAD_DIM * h, HEAD_DIM)[...] = dk
                own_kv(r, lw + HEAD_DIM * h, HEAD_DIM)[...] = dv
            else:
                chunk[feats, :] = dk.astype(bf16)
                chunk[more, :] = dv.astype(bf16)
        if not keep:
            store_chunk(r, block)

    def back_far(r):
        prepare(r)
        if small:
            attend_back(r, b ^ 3, False)
            kv_folds[r].across(0).start()
            kv_folds[r].across(1).start()
        else:

            def body(k):
                attend_back(r, b ^ k, False)
                kv_folds[r].start_one(k)

            each(1, dm.nb, body)

    def back_near(r, half):
        if small:
            attend_back(r, b ^ (half + 1), False)
            kv_folds[r].near(half).start()

    def fold_kv(r):
        if small:
            kv_folds[r].fold(0)
            kv_folds[r].fold(1)

    def project_back(r):
        if small:
            for half in (0, 1):
                kv_folds[r].wait(half)
                own_kv(r, lw * half, lw)[...] += kv_folds[r].received(half)
        else:

            def add(k):
                kv_folds[r].wait(k)
                sync(R.dkv_r.at[r, b ^ k], R.kvc)
                own_kv(r, 0, 2 * lw)[...] += R.kvc[...].astype(f32)

            each(1, dm.nb, add)
        R.low_s[r, 0:lw, :] = (dq_at(r, 0, lw)[...] * HEAD_DIM**-0.5).astype(bf16)
        R.low_s[r, lw:, :] = own_kv(r, 0, 2 * lw)[...].astype(bf16)
        R.tp_s[r] = back_through(R.wN, R.low_s[r], lw).astype(bf16)
        R.tp_s[r, :, cut(t, pt)] = (back_through(R.wN, R.low_s[r, :, cut(t, pt)], lw) + R.frT[r]).astype(bf16)
        tok_folds[r].start()

    def weight_grads(r):
        ones = jnp.ones((16, tok), bf16)
        for n, m in ((0, 0), (1, 2)):
            sums = dot(ones, R.low_s[r, pl.ds(lw * m, lw), :], 1, 1)
            if r == 0:
                R.bv_s[0, n : n + 1, 0:lw] = sums[:1]
            else:
                R.bv_s[0, n : n + 1, 0:lw] += sums[:1]
        grads = dot(R.low_s[r], R.xT[r], 1, 1)
        if r == 0:
            R.w_acc[...] = grads
        else:
            R.w_acc[...] += grads

    def add_up(first, parts, n):
        result = first.astype(f32)
        for k in range(n):
            result = result + parts(k)
        return result

    def fold_first(n):
        first_stage[n].fold(0)
        first_stage[n].fold(1)

    def reduce_first(n):
        for half in (0, 1):
            first_stage[n].wait(half)
            part = parts[n](b, half)
            part[...] = (part[...].astype(f32) + first_stage[n].received(half)).astype(bf16)
        second_stage[n].start()

    def group_sum(ref, got):
        ref[...] = add_up(ref[...], lambda k: got[(b ^ (4 * (k + 1))) // 4].astype(f32), groups - 1).astype(bf16)

    def across_groups(swap, ref, got):
        if groups > 1:
            swap.start()
            swap.wait_all()
            swap.done()
            group_sum(ref, got)

    def others_sum(got):
        return lambda k: got[lax.rem(t + 1 + k, z)].astype(f32)

    def reduce_second(n):
        own = (
            lambda: R.uG[cut(q, dm.uq), cut(t, hf)],
            lambda: R.dG[t, cut(q, dm.dq), :],
            lambda: R.oG[t, cut(q, dm.oq), :],
        )[n]
        sums = (R.u_f, R.d_f, R.o_f)[n]
        sums[...] = own().astype(f32)

        def add(ref):
            sums[...] += ref[...].astype(f32)

        second_stage[n].finish(add)
        piece_refs[n][...] = sums[...].astype(bf16)
        across_groups(group_stage[n], piece_refs[n], group_refs[n])
        place_copies[n].start()
        third_stage[n].start()

    def tokens_out(r):
        R.tgT[r] = R.tp_s[r, cut(t, lw), :].astype(f32)

        def add(ref):
            R.tgT[r] += ref[...].astype(f32)

        tok_folds[r].finish(add)

    def add_vec(k):
        R.vs[1] += R.vb[b ^ k]

    def add_bias(k):
        R.bvF[...] += R.bvb[b ^ k]

    back_far(0)
    back_near(0, 0)
    back_near(0, 1)
    attend_back(0, b, True)
    vec_pair.wait_all()
    R.vs[0] = R.sv[...] + R.vp[...]
    vec_blk.start()
    back_far(1)
    fold_kv(0)
    reduce_first(1)
    back_near(1, 0)
    back_near(1, 1)
    second_stage[1].step(1)
    attend_back(1, b, True)
    send_first(0)
    fold_kv(1)
    second_stage[1].step(2)
    project_back(0)
    vec_blk.wait_all()
    R.vs[1] = R.vs[0]
    each(1, dm.nb, add_vec)
    vec_z.start()
    weight_grads(0)
    tok_folds[0].step(1)
    reduce_second(1)
    fold_first(0)
    project_back(1)
    send_first(2)
    tok_folds[0].step(2)
    weight_grads(1)
    R.wT[...] = R.w_acc[...].astype(bf16)
    w_pair.start()
    bv_pair.start()
    tok_folds[1].step(1)
    third_stage[1].forward()
    w_pair.wait_all()
    R.w1[...] = (R.w_acc[cut(c, half_w), :] + R.wR[...].astype(f32)).astype(bf16)
    w_blk.start()
    bv_pair.wait_all()
    R.bv_s[1] = R.bv_s[0] + R.bvp[...]
    bv_blk.start()
    fold_first(2)
    tokens_out(0)
    tok_folds[1].step(2)
    reduce_first(0)
    reduce_first(2)
    w_blk.wait_all()
    R.wP[...] = add_up(
        R.w1[cut(start_r, wq_r), cut(start_l, wq_l)], lambda k: R.wr[q ^ (k + 1)].astype(f32), 3
    ).astype(bf16)
    across_groups(w_group, R.wP, R.gw)
    w_place.start()
    w_plane.start()
    second_stage[0].step(1)
    second_stage[2].step(1)
    tokens_out(1)
    w_plane.forward()
    second_stage[0].step(2)
    second_stage[2].step(2)
    vec_z.wait_all()
    R.svF[...] = add_up(R.vs[1], others_sum(R.vz), z - 1)
    bv_blk.wait_all()
    R.bvF[...] = R.bv_s[1]
    each(1, dm.nb, add_bias)
    reduce_second(0)
    reduce_second(2)
    third_stage[0].forward()
    third_stage[2].forward()
    order = (
        (third_stage[1], place_copies[1], last_stage[1]),
        (w_plane, w_place, w_last),
        (third_stage[0], place_copies[0], last_stage[0]),
        (third_stage[2], place_copies[2], last_stage[2]),
    )
    for gather, copy, swap in order:
        copy.wait()
        gather.wait_all()
        swap.start()
    for _, _, swap in order:
        swap.wait_all()
    for swap in out_swaps:
        swap.wait_all()
    for transfer in (
        up_spread, down_spread, *ctx_swaps, cot_swap, ub_swap, seg_swap, wo_pair,
        hl_pair, feed_pair, fg_pair, part_pair, og_pair, *out_swaps, *grad_swaps,
        *first_stage, *second_stage, *third_stage, *last_stage, vec_pair, vec_blk, vec_z, bv_pair, bv_blk,
        *kv_folds, *tok_folds, w_pair, w_blk, w_plane, w_last,
    ):
        transfer.done()


def back_through(w, low, lw):
    return sum(dot(w[m], low[lw * m : lw * (m + 1)], 1, 0) for m in range(3))


def run_layer(dm, *inputs):
    shape = jax.ShapeDtypeStruct
    vmem, hbm = pl.BlockSpec(memory_space=pltpu.VMEM), pl.BlockSpec(memory_space=pl.ANY)
    V, rows, lw, tok, d, pt, own, z = pltpu.VMEM, dm.rows, dm.lw, dm.tok, dm.d, dm.pt, dm.own, dm.z
    small = dm.nb == 4
    both, half_h, half_z = 2 * own, dm.hid // 2, z // 2
    vectors = [f"vec{n}" for n in range(7)]
    in_names = ["tok", "seg", "w", "ib", "cot", *vectors, "up", "down", "wo"]
    outs = {
        "loT": ((rows, lw, tok), bf16, vmem),
        "tgT": ((rows, lw, tok), f32, vmem),
        "wF": ((dm.wr, d), bf16, hbm),
        "fu": ((d, dm.ff), bf16, hbm),
        "fd": ((dm.ff, d), bf16, hbm),
        "fo": ((lw, d), bf16, hbm),
        "svF": ((16, d), f32, vmem),
        "bvF": ((8, 256), f32, vmem),
    }
    kv, received = ((rows, dm.nb, 2 * lw, tok), bf16), ((rows, 3 if small else dm.nb, 2 * lw, tok), bf16)
    if not small:
        outs["kv"], outs["dkv_r"] = (*kv, hbm), (*received, hbm)
    scratch = {
        "xT": V((rows, d, tok), bf16),
        "wT": V((dm.wr, d), bf16),
        "wN": V((3, d, lw), bf16),
        "bcol": V((2, lw, 128), f32),
        "vec": V((8, d), f32),
        "qT": V((rows, lw, tok), bf16),
        "segg": V((dm.nb, 8, tok), jnp.int32),
        "m_s": V((rows, dm.heads, 8, tok), f32),
        "l_s": V((rows, dm.heads, 8, tok), f32),
        "acc": V((rows, dm.heads, HEAD_DIM, tok), f32),
        "ctxr": V((rows, lw, tok), f32),
        "ctxs": V((rows, lw, tok), bf16),
        "ctxT": V((rows, d, pt), bf16),
        "cotT": V((rows, d, pt), bf16),
        "lse": V((rows, 8, tok), f32),
        "ub8": V((8, dm.hf), f32),
        "ubH": V((8, dm.hid), f32),
        "upH": V((d, dm.hid), bf16),
        "downH": V((z, dm.hf, d), bf16),
        "woF": V((z, lw, d), bf16),
        "hl": V((both, d), bf16),
        "act": V((both, dm.hid), bf16),
        "bg": V((both, dm.hid), bf16),
        "pool": V((dm.hid // tok * both, tok), f32),
        "fgf": V((both, d), bf16),
        "fs_s": V((2, own, d), bf16),
        "fs_r": V((2, own, d), bf16),
        "z1_s": V((own, d), f32),
        "srg_s": V((own, d), f32),
        "outT": V((rows, d, pt), bf16),
        "cgT": V((rows, d, pt), bf16),
        "og_s": V((z, lw, dm.ol), bf16),
        "og_r": V((z, lw, dm.ol), bf16),
        "doT": V((rows, lw, tok), bf16),
        "frT": V((rows, d, pt), f32),
        "dG": V((z, dm.hf, d), bf16),
        "uG": V((d, dm.hid), bf16),
        "oG": V((z, lw, dm.ol), bf16),
        "sv": V((16, d), f32),
        "low_s": V((rows, 3 * lw, tok), bf16),
        "delta": V((rows, 8, tok), f32),
        "tp_s": V((rows, d, tok), bf16),
        "tp_r": V((rows, z + 1, lw, tok), bf16),
        "ur": V((6, dm.uq, half_h), bf16),
        "dr": V((6, half_z, dm.dq, d), bf16),
        "orr": V((6, half_z, dm.oq, dm.ol), bf16),
        "u2": V((z + 1, dm.uq, dm.hf), bf16),
        "d2": V((z + 1, dm.dq, d), bf16),
        "o2": V((z + 1, dm.oq, dm.ol), bf16),
        "u_f": V((dm.uq, dm.hf), f32),
        "d_f": V((dm.dq, d), f32),
        "o_f": V((dm.oq, dm.ol), f32),
        "uP": V((dm.uq, dm.hf), bf16),
        "dP": V((dm.dq, d), bf16),
        "oP": V((dm.oq, dm.ol), bf16),
        "wP": V((dm.wr // 4, d // 2), bf16),
        "vp": V((16, d), f32),
        "vb": V((dm.nb, 16, d), f32),
        "vz": V((z, 16, d), f32),
        "vs": V((2, 16, d), f32),
        "wR": V((dm.wr // 2, d), bf16),
        "w1": V((dm.wr // 2, d), bf16),
        "wr": V((4, dm.wr // 4, d // 2), bf16),
        "bv_s": V((2, 8, 256), f32),
        "bvp": V((8, 256), f32),
        "bvb": V((dm.nb, 8, 256), f32),
        "w_acc": V((dm.wr, d), f32),
        "gu": V((dm.nb // 4, dm.uq, dm.hf), bf16),
        "gd": V((dm.nb // 4, dm.dq, d), bf16),
        "go": V((dm.nb // 4, dm.oq, dm.ol), bf16),
        "gw": V((dm.nb // 4, dm.wr // 4, d // 2), bf16),
        "kvc": V((2 * lw, tok), bf16),
        "local": pltpu.SemaphoreType.DMA((8,)),
        "sems": pltpu.SemaphoreType.DMA((540 + 24 * dm.nb,)),
    }
    if small:
        scratch["kv"], scratch["dkv_r"] = V(*kv), V(*received)
    names = (*in_names, *outs, *scratch)
    return pl.pallas_call(
        functools.partial(layer_kernel, dm, names),
        name="encoder_layer",
        out_shape=[shape(s, dtype) for s, dtype, _ in outs.values()],
        in_specs=[vmem] * 12 + [hbm] * 3,
        out_specs=[spec for _, _, spec in outs.values()],
        scratch_shapes=list(scratch.values()),
        compiler_params=pltpu.CompilerParams(
            collective_id=0, has_side_effects=True, vmem_limit_bytes=VMEM_LIMIT
        ),
    )(*inputs)


def shards(
    mesh, tokens, segment_ids, input_weight, input_bias, output_weight, output_bias, first_gain, first_shift,
    up_weight, up_bias, down_weight, down_bias, second_gain, second_shift, cotangent,
):
    dm = Dims(mesh, *tokens.shape, up_weight.shape[1])
    tokT = jnp.transpose(tokens, (0, 2, 1))
    cotT = jnp.transpose(cotangent, (0, 2, 1))
    loT, tgT, wF, fu, fd, fo, svF, bvF, *_ = run_layer(
        dm, tokT, segment_ids, jnp.transpose(input_weight, (0, 2, 1)), input_bias, cotT,
        output_bias, first_gain, first_shift, down_bias, second_gain, second_shift, up_bias,
        up_weight, down_weight, output_weight,
    )
    low = write_outputs(dm, loT, tgT, wF, fu, fd, fo, svF, bvF)
    layer_output, tokens_grad, w_grad, out_w, up_w, down_w, bias, ub, *vectors = low
    second_gain_g, second_shift_g, down_b, first_gain_g, first_shift_g, out_b = vectors
    return (
        jnp.transpose(layer_output, (0, 2, 1)),
        jnp.transpose(tokens_grad, (0, 2, 1)),
        jnp.transpose(w_grad, (0, 2, 1)),
        bias,
        out_w,
        out_b,
        first_gain_g,
        first_shift_g,
        up_w,
        ub,
        down_w,
        down_b,
        second_gain_g,
        second_shift_g,
    )


def output_kernel(dm, loT, tgT, wF, fu, fd, fo, svF, bvF, lo, tg, w_o, fo_o, fu_o, fd_o, bias, ub, *vectors):
    lo[...] = loT[...]
    tg[...] = tgT[...]
    w_o[...] = wF[...].reshape(3, dm.lw, dm.d).astype(f32)
    fu_o[...] = fu[...].astype(f32)
    fd_o[...] = fd[...].astype(f32)
    fo_o[...] = fo[...].astype(f32)
    bias[...] = bvF[0:2, 0 : dm.lw]
    for n, ref in enumerate(vectors):
        ref[...] = svF[n, :]
    t = lax.axis_index("tensor")
    for half in range(2):
        row = svF[pl.ds(6 + 2 * half + lax.div(t, 2), 1), cut(lax.rem(t, 2), dm.hf)]
        ub[pl.ds(dm.hf * half, dm.hf)] = row.reshape(dm.hf)


def write_outputs(dm, *inputs):
    shape = jax.ShapeDtypeStruct
    vmem = pl.BlockSpec(memory_space=pltpu.VMEM)
    outs = [
        shape((dm.rows, dm.lw, dm.tok), bf16),
        shape((dm.rows, dm.lw, dm.tok), f32),
        shape((3, dm.lw, dm.d), f32),
        shape((dm.lw, dm.d), f32),
        shape((dm.d, dm.ff), f32),
        shape((dm.ff, dm.d), f32),
        shape((2, dm.lw), f32),
        shape((dm.ff,), f32),
        *[shape((dm.d,), f32)] * 6,
    ]
    return pl.pallas_call(
        functools.partial(output_kernel, dm),
        name="write_outputs",
        out_shape=outs,
        in_specs=[vmem] * len(inputs),
        out_specs=[vmem] * len(outs),
        compiler_params=pltpu.CompilerParams(vmem_limit_bytes=VMEM_LIMIT),
    )(*inputs)


def solution(mesh):
    rows = P("dp", "blk", "tensor")
    placed = (
        rows, P("dp", "blk"), P(None, None, "tensor"), P(None, "tensor"), P("tensor", None), P(), P(), P(),
        P(None, "tensor"), P("tensor"), P("tensor", None), P(), P(), P(), rows,
    )
    results = (
        rows, rows, P(None, None, "tensor"), P(None, "tensor"), P("tensor", None), P(), P(), P(),
        P(None, "tensor"), P("tensor"), P("tensor", None), P(), P(), P(),
    )
    return jax.shard_map(
        functools.partial(shards, mesh), mesh=mesh, in_specs=placed, out_specs=results, check_vma=False
    )
```

profile of v0, /device:TPU:1, one launch (start us, length us, event | category | flops | bytes accessed | tf_op | source)
XLA Modules:
  0.0 210.4 jit_solution(6663295414610574380)
XLA Ops:
  0.7 203.5 %encoder_layer.1 = (bf16[2,192,512]{2,1,0:T(8,128)(2,1)}, f32[2,192,512]{2,1,0:T(8,128)}, bf16[576,768]{1,0:T(8,128)(2,1)}, bf16[768,768]{1,0:T(8,128)(2,1)}, bf...) custom-call(bf16[2,192,512]{2,1,0:T(8,128)(2,1)} %bitcast.7, ...), custom_call_target="tpu_custom_call" | custom-call | tf_op jit(solution)/shard_map/encoder_layer/pallas_call | solution.py:1248
  204.2 5.8 %write_outputs.1 = (bf16[2,192,512]{2,1,0:T(8,128)(2,1)}, f32[2,192,512]{2,1,0:T(8,128)}, f32[3,192,768]{2,1,0:T(8,128)}, f32[192,768]{1,0:T(8,128)}, f32[768,76...) custom-call(bf16[2,192,512]{2,1,0:T(8,128)(2,1)} %get-tuple-element., ...), custom_call_target="tpu_custom_call" | custom-call | tf_op jit(solution)/shard_map/write_outputs/pallas_call | solution.py:1324
where the time goes:
time: 215 us; the launch traced here: 210 us
  Pallas kernels  209 us (97%)
    pallas_call x1, Pallas kernels, run_layer(): pl.pallas_call(functools.partial(layer_kernel, dm, names), name='encoder_...  204 us
    pallas_call x1, Pallas kernels, write_outputs(): pl.pallas_call(functools.partial(output_kernel, dm), name='write_outputs'...  5.8 us

commit v1 on v0

--- a/solution.py
+++ b/solution.py
@@ -836,26 +836,24 @@
             grad = dot(R.fgf[part, :], R.downH[...].reshape(dm.hid, d)[tok * n : tok * (n + 1)], 1, 1)
             R.bg[part, cols] = (grad * R.pool[cut(2 * n + core, own), :]).astype(bf16)
 
-    contract(c)
-    fg_pair.wait_all()
-    contract(1 - c)
-    R.fs_s[1] = dot(R.bg[other, :], R.upH[...], 1, 1).astype(bf16)
-    part_pair.start()
-    part = dot(R.bg[mine, :], R.upH[...], 1, 1)
-    for r in range(rows):
-        R.outT[r] = jnp.transpose(out[pt * r : pt * (r + 1)]).astype(bf16)
-        R.loT[r, :, cut(t, pt)] = R.outT[r, cut(t, lw), :]
-        out_swaps[r].start()
-
     def send_first(n):
         for half in (0, 1):
             first_stage[n].across(half).start()
         for half in (0, 1):
             first_stage[n].near(half).start()
 
+    contract(c)
+    fg_pair.wait_all()
     for n in range(z):
         R.dG[n] = dot(R.act[:, pl.ds(hf * n, hf)], R.fgf[...], 0, 0).astype(bf16)
     send_first(1)
+    contract(1 - c)
+    R.fs_s[1] = dot(R.bg[other, :], R.upH[...], 1, 1).astype(bf16)
+    part_pair.start()
+    part = dot(R.bg[mine, :], R.upH[...], 1, 1)
+    for n in range(blocks):
+        cols = pl.ds(tok * n, tok)
+        R.uG[:, cols] = dot(R.hl[...], R.bg[:, cols], 0, 0).astype(bf16)
     part_pair.wait_all()
     hidden_grad = R.srg_s[...] + (part + R.fs_r[1].astype(f32))
     z1 = R.z1_s[...]
@@ -866,25 +864,26 @@
         R.doT[r, :, cut(t, pt)] = R.cgT[r, cut(t, lw), :]
         grad_swaps[r].start()
         R.frT[r] = jnp.transpose(first[pt * r : pt * (r + 1)])
-    R.sv[3:4, :] = total(hidden_grad * z1)
-    R.sv[4:5, :] = total(hidden_grad)
-    R.sv[5:6, :] = total(low.astype(f32))
+    first_stage[1].fold(0)
+    first_stage[1].fold(1)
     out_grad = sum(dot(R.ctxT[r], low[pt * r : pt * (r + 1)], 1, 0) for r in range(rows))
     left = out_grad[:, : dm.ol].reshape(z, lw, dm.ol)
     right = out_grad[:, dm.ol :].reshape(z, lw, dm.ol)
     R.oG[...] = jnp.where(c == 0, left, right).astype(bf16)
     R.og_s[...] = jnp.where(c == 0, right, left).astype(bf16)
     og_pair.start()
-    for n in range(blocks):
-        cols = pl.ds(tok * n, tok)
-        R.uG[:, cols] = dot(R.hl[...], R.bg[:, cols], 0, 0).astype(bf16)
+    R.sv[3:4, :] = total(hidden_grad * z1)
+    R.sv[4:5, :] = total(hidden_grad)
+    R.sv[5:6, :] = total(low.astype(f32))
     for n in range(z):
         R.sv[pl.ds(6 + 2 * c + n // 2, 1), pl.ds(hf * (n % 2), hf)] = total(
             R.bg[:, pl.ds(hf * n, hf)].astype(f32)
         )
     vec_pair.start()
-    first_stage[1].fold(0)
-    first_stage[1].fold(1)
+    for r in range(rows):
+        R.outT[r] = jnp.transpose(out[pt * r : pt * (r + 1)]).astype(bf16)
+        R.loT[r, :, cut(t, pt)] = R.outT[r, cut(t, lw), :]
+        out_swaps[r].start()
     og_pair.wait_all()
     R.oG[...] = (R.oG[...].astype(f32) + R.og_r[...].astype(f32)).astype(bf16)
 

time: 215 us -> 212 us (0.986)
    pallas_call x1, Pallas kernels: 204 us -> 201 us  [run_layer(): pl.pallas_call(functools.partial(layer_kernel, dm, names), name='encoder_...]
where the time goes in v1:
time: 212 us; the launch traced here: 208 us
  Pallas kernels  207 us (98%)
    pallas_call x1, Pallas kernels, run_layer(): pl.pallas_call(functools.partial(layer_kernel, dm, names), name='encoder_...  201 us
    pallas_call x1, Pallas kernels, write_outputs(): pl.pallas_call(functools.partial(output_kernel, dm), name='write_outputs'...  5.8 us

profile of v1, /device:TPU:1, one launch (start us, length us, event | category | flops | bytes accessed | tf_op | source)
XLA Modules:
  0.0 208.3 jit_solution(7598461506896844206)
XLA Ops:
  0.7 201.4 %encoder_layer.1 = (bf16[2,192,512]{2,1,0:T(8,128)(2,1)}, f32[2,192,512]{2,1,0:T(8,128)}, bf16[576,768]{1,0:T(8,128)(2,1)}, bf16[768,768]{1,0:T(8,128)(2,1)}, bf...) custom-call(bf16[2,192,512]{2,1,0:T(8,128)(2,1)} %bitcast.7, ...), custom_call_target="tpu_custom_call" | custom-call | tf_op jit(solution)/shard_map/encoder_layer/pallas_call | solution.py:1247
  202.0 5.8 %write_outputs.1 = (bf16[2,192,512]{2,1,0:T(8,128)(2,1)}, f32[2,192,512]{2,1,0:T(8,128)}, f32[3,192,768]{2,1,0:T(8,128)}, f32[192,768]{1,0:T(8,128)}, f32[768,76...) custom-call(bf16[2,192,512]{2,1,0:T(8,128)(2,1)} %get-tuple-element., ...), custom_call_target="tpu_custom_call" | custom-call | tf_op jit(solution)/shard_map/write_outputs/pallas_call | solution.py:1323

commit v2 on v1

--- a/solution.py
+++ b/solution.py
@@ -1062,9 +1062,10 @@
     back_near(1, 0)
     back_near(1, 1)
     second_stage[1].step(1)
+    send_first(0)
     attend_back(1, b, True)
-    send_first(0)
     fold_kv(1)
+    send_first(2)
     second_stage[1].step(2)
     project_back(0)
     vec_blk.wait_all()
@@ -1076,7 +1077,6 @@
     reduce_second(1)
     fold_first(0)
     project_back(1)
-    send_first(2)
     tok_folds[0].step(2)
     weight_grads(1)
     R.wT[...] = R.w_acc[...].astype(bf16)

time: 212 us -> 212 us (level)
  no operation moved by 1% of the time
where the time goes in v2:
time: 212 us; the launch traced here: 208 us
  Pallas kernels  207 us (98%)
    pallas_call x1, Pallas kernels, run_layer(): pl.pallas_call(functools.partial(layer_kernel, dm, names), name='encoder_...  201 us
    pallas_call x1, Pallas kernels, write_outputs(): pl.pallas_call(functools.partial(output_kernel, dm), name='write_outputs'...  5.8 us

profile of v2, /device:TPU:1, one launch (start us, length us, event | category | flops | bytes accessed | tf_op | source)
XLA Modules:
  0.0 208.3 jit_solution(13319948838352634998)
XLA Ops:
  0.7 201.4 %encoder_layer.1 = (bf16[2,192,512]{2,1,0:T(8,128)(2,1)}, f32[2,192,512]{2,1,0:T(8,128)}, bf16[576,768]{1,0:T(8,128)(2,1)}, bf16[768,768]{1,0:T(8,128)(2,1)}, bf...) custom-call(bf16[2,192,512]{2,1,0:T(8,128)(2,1)} %bitcast.7, ...), custom_call_target="tpu_custom_call" | custom-call | tf_op jit(solution)/shard_map/encoder_layer/pallas_call | solution.py:1247
  202.0 5.8 %write_outputs.1 = (bf16[2,192,512]{2,1,0:T(8,128)(2,1)}, f32[2,192,512]{2,1,0:T(8,128)}, f32[3,192,768]{2,1,0:T(8,128)}, f32[192,768]{1,0:T(8,128)}, f32[768,76...) custom-call(bf16[2,192,512]{2,1,0:T(8,128)(2,1)} %get-tuple-element., ...), custom_call_target="tpu_custom_call" | custom-call | tf_op jit(solution)/shard_map/write_outputs/pallas_call | solution.py:1323
